TPU v7x, 32 devices: a whole 2x2x4 slice. The times are simulated.
32 devices in a mesh: tm: 8 (over y, x, core), tile: 4 (over z).
Axes of the slice: x: 2, y: 2, z: 4, core: 2. Of those that a mesh axis runs over, the one named last changes fastest.
Arguments:
- velocity_u: float32 [384, 2, 16, 1024], P('tm', None, None, 'tile'), may hold values from -12 to 12
- velocity_v: float32 [384, 2, 16, 1024], P('tm', None, None, 'tile'), may hold values from -12 to 12
- land_sea: int32 [16, 1024], P(None, 'tile'), may hold values 0 or 1
- bottom_level: int32 [16, 1024], P(None, 'tile'), may hold values from 0 to 2
- spacing_x: float32 [16, 1024], P(None, 'tile'), may hold values from 0.5 to 2
- spacing_y: float32 [16, 1024], P(None, 'tile'), may hold values from 0.5 to 2
Outputs:
- conversion_maps: bfloat16 [384, 2, 16, 1024], P('tm', None, None, 'tile')
- mean_map: float32 [2, 16, 1024], P(None, None, 'tile')
All inputs are finite; a program needn't handle non-finite values. No bound on the sum of `land_sea` on one device may be relied on, other than what follows from the above.
Results may differ from a plain program's by a relative error of at most 0.001.
Values sent between devices are 32-bit elements; how exact they have to be, the bound alone decides.
A program may use at most 64 MiB of HBM per device.

v0:
```python
import jax
import jax.numpy as jnp
from jax import lax
from jax.sharding import PartitionSpec as P

HALF = 24
SNAPS = 48
cutoff_freq = 1.0 / 40.0


def extended(x, sides, width):
    for axis, dim in sides:
        size, length = (lax.axis_size(axis), x.shape[dim])
        up = [(i, (i + 1) % size) for i in range(size - 1)]
        down = [(j, i) for i, j in up]
        last = lax.slice_in_dim(x, length - width, length, axis=dim)
        first = lax.slice_in_dim(x, 0, width, axis=dim)
        before = lax.ppermute(last, axis, up)
        after = lax.ppermute(first, axis, down)
        x = jnp.concatenate([before, x, after], axis=dim)
    return x


def band_matrix(count):
    out_rows = jnp.arange(count, dtype=jnp.int32)[:, None]
    in_cols = jnp.arange(count + 2 * HALF, dtype=jnp.int32)[None, :]
    offset = (in_cols - out_rows - HALF).astype(jnp.float32)
    weights = 2.0 * cutoff_freq * jnp.sinc(2.0 * cutoff_freq * offset) * jnp.sinc(offset / HALF)
    return jnp.where(jnp.abs(offset) <= HALF, weights, jnp.zeros_like(weights))


def lowpass(padded, validity, blocks, block):
    matrix = band_matrix(block)

    def one_block(block_id):
        start = block_id * block
        window = lax.dynamic_slice_in_dim(padded, start, block + 2 * HALF, 0)
        valid_part = lax.dynamic_slice_in_dim(validity, start, block + 2 * HALF, 0)
        weighted = jnp.dot(
            matrix, window, precision=lax.Precision.HIGHEST, preferred_element_type=jnp.float32
        )
        weight_sum = jnp.dot(
            matrix, valid_part, precision=lax.Precision.HIGHEST, preferred_element_type=jnp.float32
        )
        return weighted / weight_sum[:, None]

    result = lax.map(one_block, jnp.arange(blocks, dtype=jnp.int32))
    return result.reshape(blocks * block, padded.shape[1])


def wet_cells(land_sea, bottom_level, levels):
    level_ids = jnp.arange(levels, dtype=jnp.int32)[:, None, None]
    return ((land_sea[None] == 1) & (level_ids < bottom_level[None])).astype(jnp.float32)


def filter_series(series):
    length = series.shape[0]
    flattened = series.reshape(length, -1)
    padded = jnp.pad(flattened, ((HALF, HALF), (0, 0)))
    validity = jnp.pad(jnp.ones((length,), jnp.float32), (HALF, HALF))
    return lowpass(padded, validity, length // SNAPS, SNAPS).reshape(series.shape)


def shards(velocity_u, velocity_v, land_sea, bottom_level, spacing_x, spacing_y):
    block_len = velocity_u.shape[0]
    total_len = block_len * lax.axis_size("tm")
    stacked = jnp.stack([velocity_u, velocity_v], axis=1)
    full_shape = stacked.shape
    flat_cells = stacked.reshape(block_len, 2, -1)
    series_mean = filter_series(
        lax.all_to_all(flat_cells, "tm", split_axis=2, concat_axis=0, tiled=True)
    )
    mean_flat = lax.all_to_all(series_mean, "tm", split_axis=0, concat_axis=2, tiled=True)
    mean_flow = mean_flat.reshape(full_shape)
    eddies = stacked - mean_flow
    wet_mask = wet_cells(land_sea, bottom_level, full_shape[2])
    masked = mean_flow * wet_mask[None, None]
    edge_cols = jnp.concatenate([masked[..., :1], masked[..., -1:]], axis=4)
    edge_ext = extended(edge_cols, (("tile", 4),), 1)
    left_col = edge_ext[..., :1]
    right_col = edge_ext[..., 3:4]
    ahead = jnp.concatenate([masked[..., 1:], right_col], axis=4)
    behind = jnp.concatenate([left_col, masked[..., :-1]], axis=4)
    grad_x = (ahead - behind) * (0.5 / spacing_x)
    row_padded = jnp.pad(masked, ((0, 0), (0, 0), (0, 0), (1, 1), (0, 0)))
    grad_y = (row_padded[..., 2:, :] - row_padded[..., :-2, :]) * (0.5 / spacing_y)
    eddy_u = eddies[:, 0]
    eddy_v = eddies[:, 1]
    total = (
        eddy_u * eddy_u * grad_x[:, 0]
        + eddy_u * eddy_v * (grad_y[:, 0] + grad_x[:, 1])
        + eddy_v * eddy_v * grad_y[:, 1]
    )
    conversion = -wet_mask[None] * total
    summed = lax.psum(jnp.sum(conversion, axis=0), "tm")
    return (conversion.astype(jnp.bfloat16), summed / total_len)


def solution(mesh):
    in_specs = (
        P("tm", None, None, "tile"),
        P("tm", None, None, "tile"),
        P(None, "tile"),
        P(None, "tile"),
        P(None, "tile"),
        P(None, "tile"),
    )
    out_specs = (P("tm", None, None, "tile"), P(None, None, "tile"))
    return jax.shard_map(shards, mesh=mesh, in_specs=in_specs, out_specs=out_specs, check_vma=False)
```

profile of v0, /device:TPU:0, one launch (start us, length us, event | category | flops | bytes accessed | tf_op | source)
XLA Modules:
  0.0 262.7 jit_solution(6098952019784487532)
XLA Ops:
  0.6 2.7 %stack.18 = f32[48,1,8192]{2,0,1:T(8,128)} reshape(f32[48,2,16,256]{3,2,1,0:T(8,128)} %param.9) | data formatting | bytes 3145728 | tf_op jit(solution)/shard_map/stack | solution.py:67
  3.3 1.4 stack.19
  4.8 2.1 pad_maximum_fusion
  6.9 8.0 %copy.21 = f32[48,2,8192]{0,1,2:T(2,128)} copy(f32[48,2,8192]{2,0,1:T(8,128)S(1)} %pad_maximum_fusion) | data formatting | bytes 6291456 | tf_op jit(solution)/shard_map/stack | solution.py:67
  14.9 16.2 %reshape.50 = f32[8,1,98304]{2,1,0:T(1,128)} reshape(f32[8192,2,48]{2,1,0:T(2,128)} %bitcast.49) | data formatting | bytes 6291456
  31.0 5.4 %all-to-all-start = ((f32[8,1,98304]{2,1,0:T(1,128)}), f32[8,1,98304]{2,1,0:T(1,128)S(1)}, u32[]{:S(2)}, u32[]{:S(2)}) async-start(f32[8,1,98304]{2,1,0:T(1,128)} %reshape.50), calls=%async_computation | async-start | bytes 6291456 | tf_op jit(solution)/shard_map/all_to_all | solution.py:71
  37.2 36.8 %all-to-all-done = f32[8,1,98304]{2,1,0:T(1,128)S(1)} async-done(((f32[8,1,98304]{2,1,0:T(1,128)}), f32[8,1,98304]{2,1,0:T(1,128)S(1)}, u32[]{:S(2)}, u32[]{:S(2)}) %all-to-all-start) | async-done | bytes 3145760 | tf_op jit(solution)/shard_map/all_to_all | solution.py:71
  74.6 11.2 %reduce = f32[8,98304]{1,0:T(8,128)} reduce(f32[8,1,98304]{2,1,0:T(1,128)S(1)} %all-to-all-done, f32[]{:T(128)} %broadcast.65), dimensions={1}, to_apply=%all_to_all.22.reduce_sub_computation | reduce | bytes 6291460 | tf_op jit(solution)/shard_map/all_to_all | solution.py:71
  85.8 19.3 %reshape.51 = f32[8192,2,48]{2,1,0:T(2,128)} reshape(f32[8,98304]{1,0:T(8,128)} %reduce) | data formatting | bytes 6291456
  105.1 7.0 %copy.30 = f32[48,2,8,1024]{3,2,0,1:T(8,128)S(1)} copy(f32[48,2,8,1024]{0,1,3,2:T(2,128)} %bitcast.50) | data formatting | bytes 6291456 | tf_op jit(solution)/shard_map/all_to_all | solution.py:71
  112.1 2.4 copy.23
  114.5 1.4 copy.31
  116.3 34.3 %while.11 = (s32[]{:T(128)}, f32[8,48,2048]{2,1,0:T(8,128)}, s32[8]{0:T(128)S(1)}, f32[432,2048]{1,0:T(8,128)S(1)}, f32[48,96]{1,0:T(8,128)}, /*index=5*/f32[432...) while((s32[]{:T(128)}, f32[8,48,2048]{2,1,0:T(8,128)}, s32[8]{0:T(128)S(1)}, ...), condition=%wide.region_1.3_spmd.clone, body=%wide.region_0.2_spmd.clone.sunk | while | flops 113399816 | bytes 1224551 | solution.py:47
  117.6 0.9 convolution_bitcast_fusion.2
  118.5 2.1 fusion.59
  121.9 0.9 convolution_bitcast_fusion.2
  122.9 2.1 fusion.59
  126.2 0.9 convolution_bitcast_fusion.2
  127.1 2.1 fusion.59
  130.5 0.9 convolution_bitcast_fusion.2
  131.4 2.1 fusion.59
  134.8 0.9 convolution_bitcast_fusion.2
  135.7 2.1 fusion.59
  139.0 0.9 convolution_bitcast_fusion.2
  140.0 2.1 fusion.59
  143.3 0.9 convolution_bitcast_fusion.2
  144.3 2.1 fusion.59
  147.6 0.9 convolution_bitcast_fusion.2
  148.5 2.1 fusion.59
  150.6 5.6 %reshape_reshape.3 = f32[384,2,1024]{2,1,0:T(2,128)} reshape(f32[8,48,2048]{2,1,0:T(8,128)} %get-tuple-element.38) | data formatting | bytes 6291456 | tf_op jit(solution)/shard_map/reshape;reshape | solution.py:61
  156.2 4.0 %all-to-all-start.1 = ((f32[384,2,1024]{2,1,0:T(2,128)}), f32[384,2,1024]{2,1,0:T(2,128)S(1)}, u32[]{:S(2)}, u32[]{:S(2)}) async-start(f32[384,2,1024]{2,1,0:T(2,128)} %reshape_reshape.3), calls=%async_computation.1 | async-start | bytes 6291456 | tf_op jit(solution)/shard_map/all_to_all | solution.py:73
  160.3 37.7 %all-to-all-done.1 = f32[384,2,1024]{2,1,0:T(2,128)S(1)} async-done(((f32[384,2,1024]{2,1,0:T(2,128)}), f32[384,2,1024]{2,1,0:T(2,128)S(1)}, u32[]{:S(2)}, u32[]{:S(2)}) %all-to-all-start.1) | async-done | bytes 3145760 | tf_op jit(solution)/shard_map/all_to_all | solution.py:73
  198.0 1.0 copy.24
  199.0 1.8 copy.25
  200.8 2.6 reshape.47
  203.4 5.7 %maximum_subtract_fusion = (f32[48,2,2,16,256]{4,3,2,1,0:T(8,128)}, f32[48,2,2,16,256]{4,3,2,1,0:T(8,128)S(1)}) fusion(f32[48,2,2,16,256]{4,3,2,1,0:T(8,128)} %reshape.47, f32[48,1,2,16,256]{4,3,2,1,0:T(8,128)} %bitcast.55, f32[48,1,2,16,256]{4,3,2,1,0:T(8,128)} %bitcast.56, f32[2,16,256]{2,1,0:T(8,128)S(1)} %fusion.15), kind=kLoop, calls=%fused_computation.12 | loop fusion | flops 2359296 | bytes 12615680 | tf_op jit(solution)/shard_map/sub | solution.py:75
  209.1 3.7 %fusion.47 = (f32[48,2,2,16,255]{4,3,2,1,0:T(8,128)}, f32[48,2,2,16,255]{4,3,2,1,0:T(8,128)}) fusion(f32[48,2,2,16,256]{4,3,2,1,0:T(8,128)S(1)} %get-tuple-element.70), kind=kLoop, calls=%fused_computation.85 | loop fusion | bytes 12533760 | tf_op jit(solution)/shard_map/slice | solution.py:83
  212.8 2.3 fusion.46
  215.1 2.2 copy.26
  217.3 1.3 collective-permute-start
  218.6 2.2 copy.28
  220.8 4.7 %collective-permute-start.1 = (f32[48,2,2,16,1]{0,3,4,2,1:T(8,128)S(1)}, f32[48,2,2,16,1]{0,3,4,2,1:T(8,128)S(1)}, u32[]{:S(2)}, u32[]{:S(2)}) collective-permute-start(f32[48,2,2,16,1]{0,3,4,2,1:T(8,128)S(1)} %copy.28), channel_id=1, source_target_pairs={{0,1},{1,2},{2,3},{4,5},{5,6},{6,7},{8,9},{9,10},{10,11},{12,13},{... | collective-permute-start | bytes 36872 | tf_op jit(solution)/shard_map/ppermute | solution.py:18
  225.5 2.4 fusion.7
  228.0 2.4 copy.27
  230.3 2.4 copy.29
  232.7 4.3 %fusion.8 = f32[48,2,2,16,256]{4,3,2,1,0:T(8,128)S(1)} fusion(f32[48,2,2,16,1]{4,3,2,1,0:T(8,128)} %copy.27, f32[48,2,2,16,255]{4,3,2,1,0:T(8,128)} %get-tuple-element.74, f32[48,2,2,16,255]{4,3,2,1,0:T(8,128)S(1)} %copy-done.2, f32[48,2,2,16,1]{4,3,2,1,0:T(8,128)} %copy.29, f32[16,256]{1,0:T(8,128)S(1)} %broadcast_divide_fusion.1), kind=kLoop, calls=%fused_computation.15 | loop fusion | flops 3145728 | bytes 9453568 | tf_op jit(solution)/shard_map/mul | solution.py:84
  237.4 2.1 fusion.44
  239.5 22.3 %psum.7 = f32[2,16,256]{2,1,0:T(8,128)S(1)} all-reduce(f32[2,16,256]{2,1,0:T(8,128)S(1)} %get-tuple-element.67), channel_id=1, replica_groups=mesh['tm'=8,'tile'=4] {'tm'}, use_global_device_ids=true, to_apply=%region_3.5 | all-reduce | flops 8192 | bytes 65536 | tf_op jit(solution)/shard_map/psum | solution.py:95
  (39 shorter events, 7.6 us)
Async XLA Ops:
  0.6 2.7 %copy-start.3 = (f32[48,2,16,256]{3,2,1,0:T(8,128)S(1)}, f32[48,2,16,256]{3,2,1,0:T(8,128)}, u32[]{:S(2)}) copy-start(f32[48,2,16,256]{3,2,1,0:T(8,128)} %param.10) | copy-start | bytes 4718596
  31.0 43.1 %all-to-all-start = ((f32[8,1,98304]{2,1,0:T(1,128)}), f32[8,1,98304]{2,1,0:T(1,128)S(1)}, u32[]{:S(2)}, u32[]{:S(2)}) async-start(f32[8,1,98304]{2,1,0:T(1,128)} %reshape.50), calls=%async_computation | async-start | bytes 6291456 | tf_op jit(solution)/shard_map/all_to_all | solution.py:71
  156.2 4.0 %copy-start.5 = (s32[16,256]{1,0:T(8,128)S(1)}, s32[16,256]{1,0:T(8,128)}, u32[]{:S(2)}) copy-start(s32[16,256]{1,0:T(8,128)} %param.11) | copy-start | bytes 49156
  156.2 4.0 %copy-start.6 = (f32[16,256]{1,0:T(8,128)S(1)}, f32[16,256]{1,0:T(8,128)}, u32[]{:S(2)}) copy-start(f32[16,256]{1,0:T(8,128)} %param.13) | copy-start | bytes 49156
  156.2 4.0 %copy-start.7 = (f32[16,256]{1,0:T(8,128)S(1)}, f32[16,256]{1,0:T(8,128)}, u32[]{:S(2)}) copy-start(f32[16,256]{1,0:T(8,128)} %param.14) | copy-start | bytes 49156
  156.2 4.1 %copy-start.4 = (s32[16,256]{1,0:T(8,128)S(1)}, s32[16,256]{1,0:T(8,128)}, u32[]{:S(2)}) copy-start(s32[16,256]{1,0:T(8,128)} %param.12) | copy-start | bytes 49156
  156.2 41.8 %all-to-all-start.1 = ((f32[384,2,1024]{2,1,0:T(2,128)}), f32[384,2,1024]{2,1,0:T(2,128)S(1)}, u32[]{:S(2)}, u32[]{:S(2)}) async-start(f32[384,2,1024]{2,1,0:T(2,128)} %reshape_reshape.3), calls=%async_computation.1 | async-start | bytes 6291456 | tf_op jit(solution)/shard_map/all_to_all | solution.py:73
  217.3 10.7 %collective-permute-start = (f32[48,2,2,16,1]{0,3,4,2,1:T(8,128)S(1)}, f32[48,2,2,16,1]{0,3,4,2,1:T(8,128)S(1)}, u32[]{:S(2)}, u32[]{:S(2)}) collective-permute-start(f32[48,2,2,16,1]{0,3,4,2,1:T(8,128)S(1)} %copy.26), channel_id=1, source_target_pairs={{1,0},{2,1},{3,2},{5,4},{6,5},{7,6},{9,8},{10,9},{11,10},{13,12},{... | collective-permute-start | bytes 36872 | tf_op jit(solution)/shard_map/ppermute | solution.py:19
  220.8 9.6 %collective-permute-start.1 = (f32[48,2,2,16,1]{0,3,4,2,1:T(8,128)S(1)}, f32[48,2,2,16,1]{0,3,4,2,1:T(8,128)S(1)}, u32[]{:S(2)}, u32[]{:S(2)}) collective-permute-start(f32[48,2,2,16,1]{0,3,4,2,1:T(8,128)S(1)} %copy.28), channel_id=1, source_target_pairs={{0,1},{1,2},{2,3},{4,5},{5,6},{6,7},{8,9},{9,10},{10,11},{12,13},{... | collective-permute-start | bytes 36872 | tf_op jit(solution)/shard_map/ppermute | solution.py:18
  228.0 4.7 %copy-start.2 = (f32[48,2,2,16,255]{4,3,2,1,0:T(8,128)S(1)}, f32[48,2,2,16,255]{4,3,2,1,0:T(8,128)}, u32[]{:S(2)}) copy-start(f32[48,2,2,16,255]{4,3,2,1,0:T(8,128)} %get-tuple-element.73) | copy-start | bytes 9400324
  232.7 4.3 %copy-start = (f32[48,2,2,16,256]{4,3,2,1,0:T(8,128)S(1)}, f32[48,2,2,16,256]{4,3,2,1,0:T(8,128)}, u32[]{:S(2)}) copy-start(f32[48,2,2,16,256]{4,3,2,1,0:T(8,128)} %fusion.7) | copy-start | bytes 9437188
  232.7 4.7 %copy-start.1 = (f32[48,2,2,16,256]{4,3,2,1,0:T(8,128)S(1)}, f32[48,2,2,16,256]{4,3,2,1,0:T(8,128)}, u32[]{:S(2)}) copy-start(f32[48,2,2,16,256]{4,3,2,1,0:T(8,128)} %get-tuple-element.69) | copy-start | bytes 9437188
where the time goes:
time: 267 us; the launch traced here: 263 us
  local copies, waits for them, and re-layouts  90.8 us (34%)
  waiting for transfers between devices  74.5 us (28%)
  other arithmetic  29.2 us (11%)
  matrix products  24.2 us (9%)
  blocking collectives  22.3 us (8%)
  starting transfers between devices  15.4 us (6%)
  loops' own time  5.18 us (2%)
    all_to_all x1, waiting for transfers between devices, shards(): lax.all_to_all(series_mean, 'tm', split_axis=0, concat_axis=2, tiled=True)  37.7 us
    unnamed x19, local copies, waits for them, and re-layouts  37.3 us
    all_to_all x1, waiting for transfers between devices, shards(): lax.all_to_all(flat_cells, 'tm', split_axis=2, concat_axis=0, tiled=True)  36.8 us
    psum x1, blocking collectives, shards(): summed = lax.psum(jnp.sum(conversion, axis=0), 'tm')  22.3 us
    dot_general x8, matrix products, one_block(): jnp.dot(matrix, window, precision=lax.Precision.HIGHEST, preferred_elemen...  16.8 us
    another operation x3, local copies, waits for them, and re-layouts, shards(): stacked = jnp.stack([velocity_u, velocity_v], axis=1)  12.1 us
    all_to_all x1, other arithmetic, shards(): lax.all_to_all(flat_cells, 'tm', split_axis=2, concat_axis=0, tiled=True)  11.2 us
    all_to_all x3, local copies, waits for them, and re-layouts, shards(): lax.all_to_all(flat_cells, 'tm', split_axis=2, concat_axis=0, tiled=True)  9.91 us
  transfers between devices with their start and end apart: 4, of which 2 were waited for; matrix products, arithmetic and copies ran while one was open for 3% of the time, Pallas kernels for 0%

commit v1 on v0

--- a/solution.py
+++ b/solution.py
@@ -92,7 +92,9 @@
         + eddy_v * eddy_v * grad_y[:, 1]
     )
     conversion = -wet_mask[None] * total
-    summed = lax.psum(jnp.sum(conversion, axis=0), "tm")
+    value = jnp.sum(conversion, axis=0)
+    terms = lax.all_gather(value, "tm")
+    summed = jnp.sum(terms, axis=0)
     return (conversion.astype(jnp.bfloat16), summed / total_len)
 
 

time: 267 us -> 253 us (0.948)
  blocking collectives: 22.3 us -> 8.32 us
    psum x1 -> x0, blocking collectives: 22.3 us -> none  [shards(): summed = lax.psum(jnp.sum(conversion, axis=0), 'tm')]
    all_gather x0 -> x1, blocking collectives: none -> 8.32 us  [shards(): terms = lax.all_gather(value, 'tm')]
where the time goes in v1:
time: 253 us; the launch traced here: 249 us
  local copies, waits for them, and re-layouts  90.8 us (36%)
  waiting for transfers between devices  74.5 us (29%)
  other arithmetic  29.2 us (12%)
  matrix products  24.2 us (10%)
  starting transfers between devices  15.4 us (6%)
  blocking collectives  8.32 us (3%)
  loops' own time  5.18 us (2%)
    all_to_all x1, waiting for transfers between devices, shards(): lax.all_to_all(series_mean, 'tm', split_axis=0, concat_axis=2, tiled=True)  37.7 us
    unnamed x19, local copies, waits for them, and re-layouts  37.3 us
    all_to_all x1, waiting for transfers between devices, shards(): lax.all_to_all(flat_cells, 'tm', split_axis=2, concat_axis=0, tiled=True)  36.8 us
    dot_general x8, matrix products, one_block(): jnp.dot(matrix, window, precision=lax.Precision.HIGHEST, preferred_elemen...  16.8 us
    another operation x3, local copies, waits for them, and re-layouts, shards(): stacked = jnp.stack([velocity_u, velocity_v], axis=1)  12.1 us
    all_to_all x1, other arithmetic, shards(): lax.all_to_all(flat_cells, 'tm', split_axis=2, concat_axis=0, tiled=True)  11.2 us
    all_to_all x3, local copies, waits for them, and re-layouts, shards(): lax.all_to_all(flat_cells, 'tm', split_axis=2, concat_axis=0, tiled=True)  9.91 us
    all_gather x1, blocking collectives, shards(): terms = lax.all_gather(value, 'tm')  8.32 us
  transfers between devices with their start and end apart: 4, of which 2 were waited for; matrix products, arithmetic and copies ran while one was open for 3% of the time, Pallas kernels for 0%

profile of v1, /device:TPU:0, one launch (start us, length us, event | category | flops | bytes accessed | tf_op | source)
XLA Modules:
  0.0 248.7 jit_solution(3495436349109585962)
XLA Ops:
  0.6 2.7 %stack.18 = f32[48,1,8192]{2,0,1:T(8,128)} reshape(f32[48,2,16,256]{3,2,1,0:T(8,128)} %param.9) | data formatting | bytes 3145728 | tf_op jit(solution)/shard_map/stack | solution.py:67
  3.3 1.4 stack.19
  4.8 2.1 pad_maximum_fusion
  6.9 8.0 %copy.21 = f32[48,2,8192]{0,1,2:T(2,128)} copy(f32[48,2,8192]{2,0,1:T(8,128)S(1)} %pad_maximum_fusion) | data formatting | bytes 6291456 | tf_op jit(solution)/shard_map/stack | solution.py:67
  14.9 16.2 %reshape.51 = f32[8,1,98304]{2,1,0:T(1,128)} reshape(f32[8192,2,48]{2,1,0:T(2,128)} %bitcast.50) | data formatting | bytes 6291456
  31.0 5.4 %all-to-all-start = ((f32[8,1,98304]{2,1,0:T(1,128)}), f32[8,1,98304]{2,1,0:T(1,128)S(1)}, u32[]{:S(2)}, u32[]{:S(2)}) async-start(f32[8,1,98304]{2,1,0:T(1,128)} %reshape.51), calls=%async_computation | async-start | bytes 6291456 | tf_op jit(solution)/shard_map/all_to_all | solution.py:71
  37.2 36.8 %all-to-all-done = f32[8,1,98304]{2,1,0:T(1,128)S(1)} async-done(((f32[8,1,98304]{2,1,0:T(1,128)}), f32[8,1,98304]{2,1,0:T(1,128)S(1)}, u32[]{:S(2)}, u32[]{:S(2)}) %all-to-all-start) | async-done | bytes 3145760 | tf_op jit(solution)/shard_map/all_to_all | solution.py:71
  74.6 11.2 %reduce = f32[8,98304]{1,0:T(8,128)} reduce(f32[8,1,98304]{2,1,0:T(1,128)S(1)} %all-to-all-done, f32[]{:T(128)} %broadcast.65), dimensions={1}, to_apply=%all_to_all.22.reduce_sub_computation | reduce | bytes 6291460 | tf_op jit(solution)/shard_map/all_to_all | solution.py:71
  85.8 19.3 %reshape.52 = f32[8192,2,48]{2,1,0:T(2,128)} reshape(f32[8,98304]{1,0:T(8,128)} %reduce) | data formatting | bytes 6291456
  105.1 7.0 %copy.30 = f32[48,2,8,1024]{3,2,0,1:T(8,128)S(1)} copy(f32[48,2,8,1024]{0,1,3,2:T(2,128)} %bitcast.51) | data formatting | bytes 6291456 | tf_op jit(solution)/shard_map/all_to_all | solution.py:71
  112.1 2.4 copy.23
  114.5 1.4 copy.31
  116.3 34.3 %while.11 = (s32[]{:T(128)}, f32[8,48,2048]{2,1,0:T(8,128)}, s32[8]{0:T(128)S(1)}, f32[432,2048]{1,0:T(8,128)S(1)}, f32[48,96]{1,0:T(8,128)}, /*index=5*/f32[432...) while((s32[]{:T(128)}, f32[8,48,2048]{2,1,0:T(8,128)}, s32[8]{0:T(128)S(1)}, ...), condition=%wide.region_1.3_spmd.clone, body=%wide.region_0.2_spmd.clone.sunk | while | flops 113399816 | bytes 1224551 | solution.py:47
  117.6 0.9 convolution_bitcast_fusion.2
  118.5 2.1 fusion.59
  121.9 0.9 convolution_bitcast_fusion.2
  122.9 2.1 fusion.59
  126.2 0.9 convolution_bitcast_fusion.2
  127.1 2.1 fusion.59
  130.5 0.9 convolution_bitcast_fusion.2
  131.4 2.1 fusion.59
  134.8 0.9 convolution_bitcast_fusion.2
  135.7 2.1 fusion.59
  139.0 0.9 convolution_bitcast_fusion.2
  140.0 2.1 fusion.59
  143.3 0.9 convolution_bitcast_fusion.2
  144.3 2.1 fusion.59
  147.6 0.9 convolution_bitcast_fusion.2
  148.5 2.1 fusion.59
  150.6 5.6 %reshape_reshape.3 = f32[384,2,1024]{2,1,0:T(2,128)} reshape(f32[8,48,2048]{2,1,0:T(8,128)} %get-tuple-element.38) | data formatting | bytes 6291456 | tf_op jit(solution)/shard_map/reshape;reshape | solution.py:61
  156.2 4.0 %all-to-all-start.1 = ((f32[384,2,1024]{2,1,0:T(2,128)}), f32[384,2,1024]{2,1,0:T(2,128)S(1)}, u32[]{:S(2)}, u32[]{:S(2)}) async-start(f32[384,2,1024]{2,1,0:T(2,128)} %reshape_reshape.3), calls=%async_computation.1 | async-start | bytes 6291456 | tf_op jit(solution)/shard_map/all_to_all | solution.py:73
  160.3 37.7 %all-to-all-done.1 = f32[384,2,1024]{2,1,0:T(2,128)S(1)} async-done(((f32[384,2,1024]{2,1,0:T(2,128)}), f32[384,2,1024]{2,1,0:T(2,128)S(1)}, u32[]{:S(2)}, u32[]{:S(2)}) %all-to-all-start.1) | async-done | bytes 3145760 | tf_op jit(solution)/shard_map/all_to_all | solution.py:73
  198.0 1.0 copy.24
  199.0 1.8 copy.25
  200.8 2.6 %reshape.47 = f32[48,2,2,16,256]{4,3,2,1,0:T(8,128)} reshape(f32[48,2,8,1024]{3,2,1,0:T(8,128)S(1)} %copy.25) | data formatting | bytes 6291456 | tf_op jit(solution)/shard_map/reshape | solution.py:74
  203.4 5.7 %maximum_subtract_fusion = (f32[48,2,2,16,256]{4,3,2,1,0:T(8,128)}, f32[48,2,2,16,256]{4,3,2,1,0:T(8,128)S(1)}) fusion(f32[48,2,2,16,256]{4,3,2,1,0:T(8,128)} %reshape.47, f32[48,1,2,16,256]{4,3,2,1,0:T(8,128)} %bitcast.56, f32[48,1,2,16,256]{4,3,2,1,0:T(8,128)} %bitcast.57, f32[2,16,256]{2,1,0:T(8,128)S(1)} %fusion.15), kind=kLoop, calls=%fused_computation.12 | loop fusion | flops 2359296 | bytes 12615680 | tf_op jit(solution)/shard_map/sub | solution.py:75
  209.1 3.7 %fusion.47 = (f32[48,2,2,16,255]{4,3,2,1,0:T(8,128)}, f32[48,2,2,16,255]{4,3,2,1,0:T(8,128)}) fusion(f32[48,2,2,16,256]{4,3,2,1,0:T(8,128)S(1)} %get-tuple-element.70), kind=kLoop, calls=%fused_computation.85 | loop fusion | bytes 12533760 | tf_op jit(solution)/shard_map/slice | solution.py:83
  212.8 2.3 fusion.46
  215.1 2.2 copy.26
  217.3 1.3 collective-permute-start
  218.6 2.2 copy.28
  220.8 4.7 %collective-permute-start.1 = (f32[48,2,2,16,1]{0,3,4,2,1:T(8,128)S(1)}, f32[48,2,2,16,1]{0,3,4,2,1:T(8,128)S(1)}, u32[]{:S(2)}, u32[]{:S(2)}) collective-permute-start(f32[48,2,2,16,1]{0,3,4,2,1:T(8,128)S(1)} %copy.28), channel_id=1, source_target_pairs={{0,1},{1,2},{2,3},{4,5},{5,6},{6,7},{8,9},{9,10},{10,11},{12,13},{... | collective-permute-start | bytes 36872 | tf_op jit(solution)/shard_map/ppermute | solution.py:18
  225.5 2.4 fusion.7
  228.0 2.4 copy.27
  230.3 2.4 copy.29
  232.7 4.3 %fusion.8 = f32[48,2,2,16,256]{4,3,2,1,0:T(8,128)S(1)} fusion(f32[48,2,2,16,1]{4,3,2,1,0:T(8,128)} %copy.27, f32[48,2,2,16,255]{4,3,2,1,0:T(8,128)} %get-tuple-element.74, f32[48,2,2,16,255]{4,3,2,1,0:T(8,128)S(1)} %copy-done.2, f32[48,2,2,16,1]{4,3,2,1,0:T(8,128)} %copy.29, f32[16,256]{1,0:T(8,128)S(1)} %broadcast_divide_fusion.1), kind=kLoop, calls=%fused_computation.15 | loop fusion | flops 3145728 | bytes 9453568 | tf_op jit(solution)/shard_map/mul | solution.py:84
  237.4 2.1 fusion.44
  239.5 8.3 %all-gather = f32[16,16,256]{2,1,0:T(8,128)S(1)} all-gather(f32[2,16,256]{2,1,0:T(8,128)S(1)} %get-tuple-element.67), channel_id=2, replica_groups=mesh['tm'=8,'tile'=4] {'tm'}, dimensions={0}, use_global_device_ids=true | all-gather | bytes 294912 | tf_op jit(solution)/shard_map/all_gather | solution.py:96
  (40 shorter events, 7.6 us)
Async XLA Ops:
  0.6 2.7 %copy-start.3 = (f32[48,2,16,256]{3,2,1,0:T(8,128)S(1)}, f32[48,2,16,256]{3,2,1,0:T(8,128)}, u32[]{:S(2)}) copy-start(f32[48,2,16,256]{3,2,1,0:T(8,128)} %param.10) | copy-start | bytes 4718596
  31.0 43.1 %all-to-all-start = ((f32[8,1,98304]{2,1,0:T(1,128)}), f32[8,1,98304]{2,1,0:T(1,128)S(1)}, u32[]{:S(2)}, u32[]{:S(2)}) async-start(f32[8,1,98304]{2,1,0:T(1,128)} %reshape.51), calls=%async_computation | async-start | bytes 6291456 | tf_op jit(solution)/shard_map/all_to_all | solution.py:71
  156.2 4.0 %copy-start.5 = (s32[16,256]{1,0:T(8,128)S(1)}, s32[16,256]{1,0:T(8,128)}, u32[]{:S(2)}) copy-start(s32[16,256]{1,0:T(8,128)} %param.11) | copy-start | bytes 49156
  156.2 4.0 %copy-start.6 = (f32[16,256]{1,0:T(8,128)S(1)}, f32[16,256]{1,0:T(8,128)}, u32[]{:S(2)}) copy-start(f32[16,256]{1,0:T(8,128)} %param.13) | copy-start | bytes 49156
  156.2 4.0 %copy-start.7 = (f32[16,256]{1,0:T(8,128)S(1)}, f32[16,256]{1,0:T(8,128)}, u32[]{:S(2)}) copy-start(f32[16,256]{1,0:T(8,128)} %param.14) | copy-start | bytes 49156
  156.2 4.1 %copy-start.4 = (s32[16,256]{1,0:T(8,128)S(1)}, s32[16,256]{1,0:T(8,128)}, u32[]{:S(2)}) copy-start(s32[16,256]{1,0:T(8,128)} %param.12) | copy-start | bytes 49156
  156.2 41.8 %all-to-all-start.1 = ((f32[384,2,1024]{2,1,0:T(2,128)}), f32[384,2,1024]{2,1,0:T(2,128)S(1)}, u32[]{:S(2)}, u32[]{:S(2)}) async-start(f32[384,2,1024]{2,1,0:T(2,128)} %reshape_reshape.3), calls=%async_computation.1 | async-start | bytes 6291456 | tf_op jit(solution)/shard_map/all_to_all | solution.py:73
  217.3 10.7 %collective-permute-start = (f32[48,2,2,16,1]{0,3,4,2,1:T(8,128)S(1)}, f32[48,2,2,16,1]{0,3,4,2,1:T(8,128)S(1)}, u32[]{:S(2)}, u32[]{:S(2)}) collective-permute-start(f32[48,2,2,16,1]{0,3,4,2,1:T(8,128)S(1)} %copy.26), channel_id=1, source_target_pairs={{1,0},{2,1},{3,2},{5,4},{6,5},{7,6},{9,8},{10,9},{11,10},{13,12},{... | collective-permute-start | bytes 36872 | tf_op jit(solution)/shard_map/ppermute | solution.py:19
  220.8 9.6 %collective-permute-start.1 = (f32[48,2,2,16,1]{0,3,4,2,1:T(8,128)S(1)}, f32[48,2,2,16,1]{0,3,4,2,1:T(8,128)S(1)}, u32[]{:S(2)}, u32[]{:S(2)}) collective-permute-start(f32[48,2,2,16,1]{0,3,4,2,1:T(8,128)S(1)} %copy.28), channel_id=1, source_target_pairs={{0,1},{1,2},{2,3},{4,5},{5,6},{6,7},{8,9},{9,10},{10,11},{12,13},{... | collective-permute-start | bytes 36872 | tf_op jit(solution)/shard_map/ppermute | solution.py:18
  228.0 4.7 %copy-start.2 = (f32[48,2,2,16,255]{4,3,2,1,0:T(8,128)S(1)}, f32[48,2,2,16,255]{4,3,2,1,0:T(8,128)}, u32[]{:S(2)}) copy-start(f32[48,2,2,16,255]{4,3,2,1,0:T(8,128)} %get-tuple-element.73) | copy-start | bytes 9400324
  232.7 4.3 %copy-start = (f32[48,2,2,16,256]{4,3,2,1,0:T(8,128)S(1)}, f32[48,2,2,16,256]{4,3,2,1,0:T(8,128)}, u32[]{:S(2)}) copy-start(f32[48,2,2,16,256]{4,3,2,1,0:T(8,128)} %fusion.7) | copy-start | bytes 9437188
  232.7 4.7 %copy-start.1 = (f32[48,2,2,16,256]{4,3,2,1,0:T(8,128)S(1)}, f32[48,2,2,16,256]{4,3,2,1,0:T(8,128)}, u32[]{:S(2)}) copy-start(f32[48,2,2,16,256]{4,3,2,1,0:T(8,128)} %get-tuple-element.69) | copy-start | bytes 9437188
